TPU v7x, 32 devices: a whole 2x2x4 slice. The times are simulated.
32 devices in a mesh: lon: 8 (over z, core), lat: 4 (over y, x).
Axes of the slice: x: 2, y: 2, z: 4, core: 2. Of those that a mesh axis runs over, the one named last changes fastest.
Arguments:
- temp: float32 [8, 1024, 4096], P(None, 'lat', 'lon'), may hold values from -6 to 6
- currents: float32 [2, 8, 1024, 4096], P(None, None, 'lat', 'lon'), may hold values from -0.4 to 0.4
- mixing: float32 [7, 1024, 4096], P(None, 'lat', 'lon'), may hold values from 0.05 to 2
- ice_vel: float32 [2, 1024, 4096], P(None, 'lat', 'lon'), may hold values from -3 to 3
- strength: float32 [1024, 4096], P('lat', 'lon'), may hold values from 0.5 to 2
- ice_list: int32 [4, 8, 8], P('lat', 'lon'), may hold values from 0 to 8, as said below
- land: int32 [16, 16], P('lat', 'lon'), may hold values 0 or 1
Outputs:
- temp_out: float32 [8, 1024, 4096], P(None, 'lat', 'lon')
- ice_vel_out: float32 [2, 1024, 4096], P(None, 'lat', 'lon')
Inputs may be any that keep to these rules, and one draw needn't show every extreme that they name: `ice_list`: each device's list holds distinct block numbers below 8, followed by entries equal to 8; the devices of one lat index list 4 * 8 blocks together, and some device of each lat index lists 8.
All inputs are finite; a program needn't handle non-finite values. No bound on the sum of `land` on one device may be relied on, other than what follows from the above.
Results may differ from a plain program's by a relative error of at most 0.00002.
Values sent between devices are 32-bit elements; how exact they have to be, the bound alone decides.
A program may use at most 128 MiB of HBM per device.

v0:
```python
import jax
import jax.numpy as jnp
from jax import lax
from jax.sharding import PartitionSpec as P

CYCLES = 32


diffusion_rate = 0.15
advect_rate = 0.5
relax_rate = 0.5
ice_step = 0.2
drag_rate = 1.0
strain_floor = 0.25
heat_rate = 0.5
freezing = -1.0


def carried_in(value, axis, join, neutral):
    count, mine = (lax.axis_size(axis), lax.axis_index(axis))
    pieces = lax.all_gather(value, axis)
    so_far = jnp.full_like(value, 0) + jnp.asarray(neutral, value.dtype)

    def lap(position, so_far):
        longer = join(so_far, pieces[position])
        return jnp.where(position < mine, longer, so_far)

    return lax.fori_loop(0, count - 1, lap, so_far)


def extended(block, sides, width):
    for axis, dim in sides:
        count = lax.axis_size(axis)
        forward = [(i, i + 1) for i in range(count - 1)]
        forward.append((count - 1, 0))
        backward = [(target, source) for source, target in forward]
        low = lax.ppermute(
            lax.slice_in_dim(block, block.shape[dim] - width, None, axis=dim), axis, forward
        )
        high = lax.ppermute(lax.slice_in_dim(block, 0, width, axis=dim), axis, backward)
        block = jnp.concatenate([low, block, high], axis=dim)
    return block


def column_mask(field, width):
    return lax.broadcasted_iota(jnp.int32, field.shape, field.ndim - 1) % width


def row_mask(field, height):
    return lax.broadcasted_iota(jnp.int32, field.shape, field.ndim - 2) % height


def east_diff(field, width):
    return jnp.where(
        column_mask(field, width) != width - 1, jnp.roll(field, -1, axis=-1) - field, 0.0
    )


def north_diff(field, height):
    return jnp.where(
        row_mask(field, height) != height - 1, jnp.roll(field, -1, axis=-2) - field, 0.0
    )


def west_diff(field, width):
    return jnp.where(column_mask(field, width) != 0, field - jnp.roll(field, 1, axis=-1), field)


def south_diff(field, height):
    return jnp.where(row_mask(field, height) != 0, field - jnp.roll(field, 1, axis=-2), field)


def subcycles(ice_u, ice_v, pressure, ocean_u, ocean_v, surface, height, width):

    def one_cycle(cycle, state):
        ice_u, ice_v, stress_one, stress_two = state
        diverge = east_diff(ice_u, width) + north_diff(ice_v, height)
        shearing = east_diff(ice_v, width) + north_diff(ice_u, height)
        delta = jnp.sqrt(diverge * diverge + shearing * shearing + strain_floor)
        viscous = pressure / (2.0 * delta)
        stress_one = (stress_one + relax_rate * (viscous * diverge - 0.5 * pressure)) / (
            1.0 + relax_rate
        )
        stress_two = (stress_two + relax_rate * viscous * shearing) / (1.0 + relax_rate)
        force_u = west_diff(stress_one, width) + south_diff(stress_two, height)
        force_v = south_diff(stress_one, height) + west_diff(stress_two, width)
        ice_u = (ice_u + ice_step * (force_u + drag_rate * ocean_u)) / (1.0 + ice_step * drag_rate)
        ice_v = (ice_v + ice_step * (force_v + drag_rate * ocean_v)) / (1.0 + ice_step * drag_rate)
        return (ice_u, ice_v, stress_one, stress_two)

    start = (ice_u, ice_v, jnp.zeros_like(ice_u), jnp.zeros_like(ice_u))
    ice_u, ice_v, stress_one, stress_two = lax.fori_loop(0, CYCLES, one_cycle, start)
    rel_u = ice_u - ocean_u
    rel_v = ice_v - ocean_v
    speed = jnp.sqrt(rel_u * rel_u + rel_v * rel_v + 0.01)
    return (ice_u, ice_v, heat_rate * speed * (freezing - surface))


def column_solve(right, mixing):
    levels = right.shape[0]
    ratios = []
    partial_value = []
    for level in range(levels):
        lower = mixing[level - 1] if level > 0 else 0.0
        upper = mixing[level] if level < levels - 1 else 0.0
        diagonal = 1.0 + lower + upper
        if level > 0:
            pivot = diagonal - lower * ratios[-1]
            value = (right[level] + lower * partial_value[-1]) / pivot
        else:
            pivot = diagonal
            value = right[level] / pivot
        ratios.append(upper / pivot)
        partial_value.append(value)
    result = [partial_value[-1]]
    for level in range(levels - 2, -1, -1):
        result.insert(0, partial_value[level] + ratios[level] * result[0])
    return jnp.stack(result)


def from_blocks(blocks, rows, cols):
    block_rows, block_cols = blocks.shape[-2:]
    shaped = blocks.reshape((rows // block_rows, cols // block_cols, block_rows, block_cols))
    shaped = jnp.moveaxis(shaped, 2, 1)
    return shaped.reshape((rows, cols))


def shards(temp, currents, mixing, ice_vel, strength, ice_list, land):
    levels, lat_cells, lon_cells = temp.shape
    lat_index = lax.axis_index("lat")
    lon_index = lax.axis_index("lon")
    lat_count = lax.axis_size("lat")
    lon_count = lax.axis_size("lon")
    block_rows = 2 * lat_cells // lon_count
    block_cols = lon_cells // 2
    cols_dev = lon_cells // block_cols
    block_total = lat_cells // block_rows * cols_dev
    owned_count = block_total // 2
    fields = (ice_vel[0], ice_vel[1], strength, currents[0, 0], currents[1, 0], temp[0])
    entries = ice_list.reshape(block_total)
    position = jnp.arange(block_total, dtype=jnp.int32)
    listed = entries < block_total
    block_match = listed[None, :] & (entries[None, :] == position[:, None])
    block_ice = jnp.any(block_match, axis=1)
    count = jnp.sum(listed.astype(jnp.int32))
    offset = carried_in(count, "lon", lambda earlier, later: earlier + later, jnp.int32(0))
    ticket = offset + position
    slot_of_entry = ticket % lon_count
    slot_ids = jnp.arange(lon_count, dtype=jnp.int32)
    slot_match = listed[None, :] & (slot_of_entry[None, :] == slot_ids[:, None])
    filled = jnp.any(slot_match, axis=1)
    entry_of_slot = jnp.sum(jnp.where(slot_match, position[None, :], 0), axis=1)
    block_of_slot = jnp.where(filled, entries[entry_of_slot], 0)

    def cut_block(field, number):
        start_row = number // cols_dev * block_rows
        start_col = number % cols_dev * block_cols
        return lax.dynamic_slice(field, (start_row, start_col), (block_rows, block_cols))

    def outgoing(field):
        pieces = jax.vmap(cut_block, (None, 0))(field, block_of_slot)
        return jnp.where(filled[:, None, None], pieces, jnp.float32(0.0))

    tickets_out = jnp.where(filled, ticket[entry_of_slot], -1).astype(jnp.int32)
    arrived = (
        lax.all_to_all(outgoing(fields[0]), "lon", split_axis=0, concat_axis=0, tiled=True),
        lax.all_to_all(outgoing(fields[1]), "lon", split_axis=0, concat_axis=0, tiled=True),
        lax.all_to_all(outgoing(fields[2]), "lon", split_axis=0, concat_axis=0, tiled=True),
        lax.all_to_all(outgoing(fields[3]), "lon", split_axis=0, concat_axis=0, tiled=True),
        lax.all_to_all(outgoing(fields[4]), "lon", split_axis=0, concat_axis=0, tiled=True),
        lax.all_to_all(outgoing(fields[5]), "lon", split_axis=0, concat_axis=0, tiled=True),
        lax.all_to_all(tickets_out, "lon", split_axis=0, concat_axis=0, tiled=True),
    )
    tickets_in = arrived[6]
    present = tickets_in >= 0
    compact_place = tickets_in // lon_count
    compact_ids = jnp.arange(owned_count, dtype=jnp.int32)
    pick = present[None, :] & (compact_place[None, :] == compact_ids[:, None])
    source = jnp.sum(jnp.where(pick, slot_ids[None, :], 0), axis=1)
    owned = subcycles(
        arrived[0][source],
        arrived[1][source],
        arrived[2][source],
        arrived[3][source],
        arrived[4][source],
        arrived[5][source],
        block_rows,
        block_cols,
    )
    back_index = jnp.clip(compact_place, 0, owned_count - 1)

    def going_back(result):
        return jnp.where(present[:, None, None], result[back_index], jnp.float32(0.0))

    returned = (
        lax.all_to_all(going_back(owned[0]), "lon", split_axis=0, concat_axis=0, tiled=True),
        lax.all_to_all(going_back(owned[1]), "lon", split_axis=0, concat_axis=0, tiled=True),
        lax.all_to_all(going_back(owned[2]), "lon", split_axis=0, concat_axis=0, tiled=True),
    )
    entry_of_block = jnp.sum(jnp.where(block_match, position[None, :], 0), axis=1)
    slot_of_block = slot_of_entry[entry_of_block]
    new_u = from_blocks(returned[0][slot_of_block], lat_cells, lon_cells)
    new_v = from_blocks(returned[1][slot_of_block], lat_cells, lon_cells)
    flux = from_blocks(returned[2][slot_of_block], lat_cells, lon_cells)
    block_grid = block_ice.reshape(lat_cells // block_rows, cols_dev)
    ice_cell = jnp.repeat(jnp.repeat(block_grid, block_rows, axis=0), block_cols, axis=1)
    land_cell = jnp.repeat(jnp.repeat(land > 0, block_rows, axis=0), block_cols, axis=1)
    ice_vel_out = jnp.where(ice_cell[None], jnp.stack([new_u, new_v]), ice_vel)
    flux_cell = jnp.where(ice_cell, flux, jnp.float32(0.0))
    top_row = temp[:, -1, :]
    whole_row = lax.all_gather(top_row, "lon", axis=1, tiled=True)
    mirrored = lax.dynamic_slice_in_dim(
        jnp.flip(whole_row, axis=1), lon_index * lon_cells, lon_cells, 1
    )
    padded = extended(temp, (("lon", 2), ("lat", 1)), 1)
    east = padded[:, 1:-1, 2:]
    west = padded[:, 1:-1, :-2]
    north = padded[:, 2:, 1:-1]
    south = padded[:, :-2, 1:-1]
    south_first = jnp.where(lat_index == 0, temp[:, :1], south[:, :1])
    south = jnp.concatenate([south_first, south[:, 1:]], axis=1)
    north_last = jnp.where(lat_index == lat_count - 1, mirrored[:, None, :], north[:, -1:])
    north = jnp.concatenate([north[:, :-1], north_last], axis=1)
    explicit = (
        temp
        + diffusion_rate * (east + west + north + south - 4.0 * temp)
        - advect_rate * (currents[0] * (east - west) + currents[1] * (north - south))
    )
    right = explicit.at[0].add(flux_cell)
    solved = column_solve(right, mixing)
    temp_out = jnp.where(land_cell[None], temp, solved)
    return (temp_out, ice_vel_out)


def solution(mesh):
    placed = (
        P(None, "lat", "lon"),
        P(None, None, "lat", "lon"),
        P(None, "lat", "lon"),
        P(None, "lat", "lon"),
        P("lat", "lon"),
        P("lat", "lon", None),
        P("lat", "lon"),
    )
    return jax.shard_map(
        shards,
        mesh=mesh,
        in_specs=placed,
        out_specs=(P(None, "lat", "lon"), P(None, "lat", "lon")),
        check_vma=False,
    )
```

profile of v0, /device:TPU:0, one launch (start us, length us, event | category | flops | bytes accessed | tf_op | source)
XLA Modules:
  0.0 435.5 jit_solution(7374770813434665192)
XLA Ops:
  5.3 10.6 %all-reduce = s32[8]{0:T(128)S(1)} all-reduce(s32[8]{0:T(128)S(1)} %dynamic-update-slice.15), channel_id=1, replica_groups=mesh['lon'=8,'lat'=4] {'lon'}, use_global_device_ids=true, to_apply=%add | all-reduce | flops 8 | bytes 64
  15.9 8.2 %while.40 = (s32[]{:T(128)}, s32[]{:T(128)}, s32[]{:T(128)}, s32[8]{0:T(128)S(1)}, s32[]{:T(128)}) while((s32[]{:T(128)}, s32[]{:T(128)}, s32[]{:T(128)}, s32[8]{0:T(128)S(1)}, s32[]{:T(128)}) %tuple.196), condition=%wide.region_3.4_spmd, body=%wide.region_2.3_spmd.sunk | while | flops 5 | bytes 115 | solution.py:28
  27.1 3.2 all-to-all-start
  33.0 16.0 %while.45 = (s32[]{:T(128)}, f32[256,512]{1,0:T(8,128)S(1)}, s32[8,2]{0,1:T(2,128)S(1)}, f32[8,64,256]{2,1,0:T(8,128)S(1)}, s32[]{:T(128)}) while((s32[]{:T(128)}, f32[256,512]{1,0:T(8,128)S(1)}, s32[8,2]{0,1:T(2,128)S(1)}, f32[8,64,256]{2,1,0:T(8,128)S(1)}, s32[]{:T(128)}) %tuple.199), condition=%wide.while_cond.5, body=%wide.while_body.5.sunk | while | flops 2 | bytes 131189 | solution.py:158
  49.9 16.0 %while.42 = (s32[]{:T(128)}, f32[256,512]{1,0:T(8,128)S(1)}, s32[8,2]{0,1:T(2,128)S(1)}, f32[8,64,256]{2,1,0:T(8,128)S(1)}, s32[]{:T(128)}) while((s32[]{:T(128)}, f32[256,512]{1,0:T(8,128)S(1)}, s32[8,2]{0,1:T(2,128)S(1)}, f32[8,64,256]{2,1,0:T(8,128)S(1)}, s32[]{:T(128)}) %tuple.220), condition=%wide.while_cond.2, body=%wide.while_body.2.sunk | while | flops 2 | bytes 131189 | solution.py:158
  66.0 23.2 %while.43 = (s32[]{:T(128)}, f32[256,512]{1,0:T(8,128)}, s32[8,2]{0,1:T(2,128)S(1)}, f32[8,64,256]{2,1,0:T(8,128)S(1)}, s32[]{:T(128)}) while((s32[]{:T(128)}, f32[256,512]{1,0:T(8,128)}, s32[8,2]{0,1:T(2,128)S(1)}, f32[8,64,256]{2,1,0:T(8,128)S(1)}, s32[]{:T(128)}) %tuple.221), condition=%wide.while_cond.3, body=%wide.while_body.3.sunk | while | flops 2 | bytes 131189 | solution.py:158
  89.3 16.1 %while.44 = (s32[]{:T(128)}, f32[256,512]{1,0:T(8,128)S(1)}, s32[8,2]{0,1:T(2,128)S(1)}, f32[8,64,256]{2,1,0:T(8,128)S(1)}, s32[]{:T(128)}) while((s32[]{:T(128)}, f32[256,512]{1,0:T(8,128)S(1)}, s32[8,2]{0,1:T(2,128)S(1)}, f32[8,64,256]{2,1,0:T(8,128)S(1)}, s32[]{:T(128)}) %tuple.222), condition=%wide.while_cond.4, body=%wide.while_body.4.sunk | while | flops 2 | bytes 131189 | solution.py:158
  106.5 15.3 %while.46 = (s32[]{:T(128)}, f32[256,512]{1,0:T(8,128)S(1)}, s32[8,2]{0,1:T(2,128)S(1)}, f32[8,64,256]{2,1,0:T(8,128)S(1)}, s32[]{:T(128)}) while((s32[]{:T(128)}, f32[256,512]{1,0:T(8,128)S(1)}, s32[8,2]{0,1:T(2,128)S(1)}, f32[8,64,256]{2,1,0:T(8,128)S(1)}, s32[]{:T(128)}) %tuple.223), condition=%wide.while_cond.6, body=%wide.while_body.6.sunk | while | flops 2 | bytes 131189 | solution.py:158
  121.9 24.1 %while.41 = (s32[]{:T(128)}, f32[256,512]{1,0:T(8,128)}, s32[8,2]{0,1:T(2,128)S(1)}, f32[8,64,256]{2,1,0:T(8,128)S(1)}, s32[]{:T(128)}) while((s32[]{:T(128)}, f32[256,512]{1,0:T(8,128)}, s32[8,2]{0,1:T(2,128)S(1)}, f32[8,64,256]{2,1,0:T(8,128)S(1)}, s32[]{:T(128)}) %tuple.224), condition=%wide.while_cond.1, body=%wide.while_body.1.sunk | while | flops 2 | bytes 131189 | solution.py:158
  122.6 2.3 bitcast_dynamic-update-slice_fusion.12
  125.6 2.3 bitcast_dynamic-update-slice_fusion.12
  128.6 2.3 bitcast_dynamic-update-slice_fusion.12
  131.6 2.3 bitcast_dynamic-update-slice_fusion.12
  134.6 2.3 bitcast_dynamic-update-slice_fusion.12
  137.6 2.3 bitcast_dynamic-update-slice_fusion.12
  140.6 2.3 bitcast_dynamic-update-slice_fusion.12
  143.6 2.3 bitcast_dynamic-update-slice_fusion.12
  147.8 5.1 %all-to-all-start.1 = ((f32[8,64,256]{2,1,0:T(8,128)}), f32[8,64,256]{2,1,0:T(8,128)S(1)}, u32[]{:S(2)}, u32[]{:S(2)}) async-start(f32[8,64,256]{2,1,0:T(8,128)} %get-tuple-element.448), calls=%async_computation.1 | async-start | bytes 1048576 | tf_op jit(solution)/shard_map/all_to_all | solution.py:166
  155.7 3.6 collective-permute-start
  160.2 8.1 %all-to-all-done.1 = f32[8,64,256]{2,1,0:T(8,128)S(1)} async-done(((f32[8,64,256]{2,1,0:T(8,128)}), f32[8,64,256]{2,1,0:T(8,128)S(1)}, u32[]{:S(2)}, u32[]{:S(2)}) %all-to-all-start.1) | async-done | bytes 524320 | tf_op jit(solution)/shard_map/all_to_all | solution.py:166
  168.3 3.5 all-to-all-start.2
  171.8 3.4 fusion.65
  175.2 8.1 %fusion.61 = (f32[1,8,256,512]{3,2,1,0:T(8,128)}, f32[1,8,256,512]{3,2,1,0:T(8,128)}) fusion(f32[2,8,256,512]{3,2,1,0:T(8,128)} %param.14), kind=kLoop, calls=%fused_computation.207 | loop fusion | bytes 16777216 | tf_op jit(solution)/shard_map/slice | solution.py:227
  183.3 3.8 all-to-all-done.2
  187.1 4.1 all-to-all-start.3
  191.3 5.3 %copy.176 = f32[8,256,512]{1,2,0:T(8,128)} copy(f32[8,256,512]{2,1,0:T(8,128)} %param.13) | data formatting | bytes 8388608 | tf_op args[0]
  196.6 6.6 %copy.153 = f32[8,256,512]{2,0,1:T(8,128)} copy(f32[8,256,512]{2,1,0:T(8,128)} %param.13) | data formatting | bytes 8388608 | tf_op args[0]
  203.2 5.4 %copy.184 = f32[1,8,256,512]{2,3,1,0:T(8,128)} copy(f32[1,8,256,512]{3,2,1,0:T(8,128)} %get-tuple-element.420) | data formatting | bytes 8388608
  208.6 5.4 %copy.183 = f32[1,8,256,512]{2,3,1,0:T(8,128)} copy(f32[1,8,256,512]{3,2,1,0:T(8,128)} %get-tuple-element.419) | data formatting | bytes 8388608
  223.3 8.0 %fusion.62 = (f32[8,255,512]{1,2,0:T(8,128)}, f32[8,255,512]{1,2,0:T(8,128)}) fusion(f32[8,256,512]{1,2,0:T(8,128)} %copy.176), kind=kLoop, calls=%fused_computation.208 | loop fusion | bytes 16711680 | tf_op jit(solution)/shard_map/slice | solution.py:223
  231.5 5.2 %all-to-all-start.4 = ((f32[8,64,256]{2,1,0:T(8,128)}), f32[8,64,256]{2,1,0:T(8,128)S(1)}, u32[]{:S(2)}, u32[]{:S(2)}) async-start(f32[8,64,256]{2,1,0:T(8,128)} %get-tuple-element.446), calls=%async_computation.4 | async-start | bytes 1048576 | tf_op jit(solution)/shard_map/all_to_all | solution.py:169
  237.4 14.7 %all-to-all-done.4 = f32[8,64,256]{2,1,0:T(8,128)S(1)} async-done(((f32[8,64,256]{2,1,0:T(8,128)}), f32[8,64,256]{2,1,0:T(8,128)S(1)}, u32[]{:S(2)}, u32[]{:S(2)}) %all-to-all-start.4) | async-done | bytes 524320 | tf_op jit(solution)/shard_map/all_to_all | solution.py:169
  252.0 4.1 all-to-all-start.5
  266.8 14.4 %all-gather = f32[8,1,4096]{2,0,1:T(8,128)S(1)} all-gather(f32[8,1,512]{2,0,1:T(8,128)S(1)} %get-tuple-element.425), channel_id=2, replica_groups=mesh['lon'=8,'lat'=4] {'lon'}, dimensions={2}, use_global_device_ids=true | all-gather | bytes 147456 | tf_op jit(solution)/shard_map/all_gather | solution.py:211
  292.6 4.5 %all-to-all-start.6 = ((f32[8,64,256]{2,1,0:T(8,128)}), f32[8,64,256]{2,1,0:T(8,128)}, u32[]{:S(2)}, u32[]{:S(2)}) async-start(f32[8,64,256]{2,1,0:T(8,128)} %get-tuple-element.447), calls=%async_computation.6 | async-start | bytes 1048576 | tf_op jit(solution)/shard_map/all_to_all | solution.py:171
  298.8 58.7 %while.47 = (s32[]{:T(128)}, f32[4,64,256]{2,1,0:T(8,128)S(1)}, f32[4,64,256]{2,1,0:T(8,128)S(1)}, f32[4,64,256]{2,1,0:T(8,128)S(1)}, f32[4,64,256]{2,1,0:T(8,12...) while((s32[]{:T(128)}, f32[4,64,256]{2,1,0:T(8,128)S(1)}, ...), condition=%wide.region_8.9_spmd.clone, body=%wide.region_7.8_spmd.clone.sunk | while | flops 4720515 | bytes 9993592 | solution.py:92
  359.5 2.4 gather_fusion.7
  363.6 2.4 broadcast_select_fusion.2
  365.9 5.1 %all-to-all-start.7 = ((f32[8,64,256]{2,1,0:T(8,128)}), f32[8,64,256]{2,1,0:T(8,128)}, u32[]{:S(2)}, u32[]{:S(2)}) async-start(f32[8,64,256]{2,1,0:T(8,128)} %get-tuple-element.442), calls=%async_computation.7 | async-start | bytes 1048576 | tf_op jit(solution)/shard_map/all_to_all | solution.py:198
  371.0 14.5 %fusion.21 = f32[8,256,512]{1,2,0:T(8,128)} fusion(f32[1,8,256,512]{2,3,1,0:T(8,128)} %copy.184, f32[1,8,256,512]{2,3,1,0:T(8,128)} %copy.183, f32[8,256,512]{1,2,0:T(8,128)} %copy.176, f32[8,255,512]{1,2,0:T(8,128)} %get-tuple-element.424, f32[8,1,512]{1,2,0:T(8,128)} %copy.160, f32[8,1,512]{1,2,0:T(8,128)} %copy.157, ...), kind=kLoop, calls=%fused_computation.73 | loop fusion | flops 18874368 | bytes 25182208 | tf_op jit(solution)/shard_map/sub | solution.py:225
  386.5 4.3 all-to-all-start.9
  390.8 2.5 gather_fusion.10
  395.6 2.3 reshape.397
  399.9 2.5 fusion.27
  411.0 5.1 %all-to-all-start.8 = ((f32[8,64,256]{2,1,0:T(8,128)}), f32[8,64,256]{2,1,0:T(8,128)}, u32[]{:S(2)}, u32[]{:S(2)}) async-start(f32[8,64,256]{2,1,0:T(8,128)} %get-tuple-element.440), calls=%async_computation.8 | async-start | bytes 1048576 | tf_op jit(solution)/shard_map/all_to_all | solution.py:196
  416.1 2.8 constant_dynamic-update-slice_fusion
  418.9 4.7 %broadcast_select_fusion = f32[8,256,512]{1,2,0:T(8,128)} fusion(f32[8,256,512]{1,2,0:T(8,128)S(1)} %copy-done, f32[8,256,512]{1,2,0:T(8,128)} %constant_dynamic-update-slice_fusion, pred[256,512]{0,1:T(8,128)(4,1)S(1)} %bitcast.187), kind=kLoop, calls=%fused_computation.75 | loop fusion | flops 1048576 | bytes 12713984 | tf_op jit(solution)/shard_map/jit(_where)/select_n | solution.py:231
  423.7 5.3 %copy.180 = f32[8,256,512]{2,1,0:T(8,128)} copy(f32[8,256,512]{1,2,0:T(8,128)} %broadcast_select_fusion) | data formatting | bytes 8388608
  (940 shorter events, 224.6 us)
Async XLA Ops:
  0.6 48.4 %copy-start.8 = (f32[2,256,512]{2,1,0:T(8,128)S(1)}, f32[2,256,512]{2,1,0:T(8,128)}, u32[]{:S(2)}) copy-start(f32[2,256,512]{2,1,0:T(8,128)} %param.16) | copy-start | bytes 3145732
  27.1 120.7 %all-to-all-start = ((s32[8,1,1]{2,1,0:T(1,128)}), s32[8,1,1]{2,1,0:T(1,128)S(1)}, u32[]{:S(2)}, u32[]{:S(2)}) async-start(s32[8,1,1]{2,1,0:T(1,128)} %copy.166), calls=%async_computation | async-start | bytes 8192 | tf_op jit(solution)/shard_map/all_to_all | solution.py:172
  147.8 12.4 %copy-start.22 = (s32[4,2]{0,1:T(2,128)S(1)}, s32[4,2]{0,1:T(2,128)}, u32[]{:S(2)}) copy-start(s32[4,2]{0,1:T(2,128)} %param.19) | copy-start | bytes 100
  147.8 20.6 %all-to-all-start.1 = ((f32[8,64,256]{2,1,0:T(8,128)}), f32[8,64,256]{2,1,0:T(8,128)S(1)}, u32[]{:S(2)}, u32[]{:S(2)}) async-start(f32[8,64,256]{2,1,0:T(8,128)} %get-tuple-element.448), calls=%async_computation.1 | async-start | bytes 1048576 | tf_op jit(solution)/shard_map/all_to_all | solution.py:166
  155.7 101.3 %collective-permute-start = (f32[8,256,1]{1,0,2:T(8,128)}, f32[8,256,1]{1,0,2:T(8,128)S(1)}, u32[]{:S(2)}, u32[]{:S(2)}) collective-permute-start(f32[8,256,1]{1,0,2:T(8,128)} %copy.181), channel_id=1, source_target_pairs={{4,0},{8,4},{12,8},{16,12},{20,16},{24,20},{28,24},{0,28},{5,1},{9... | collective-permute-start | bytes 24584 | tf_op jit(solution)/shard_map/ppermute | solution.py:40
  160.2 97.2 %collective-permute-start.1 = (f32[8,256,1]{1,0,2:T(8,128)}, f32[8,256,1]{1,0,2:T(8,128)}, u32[]{:S(2)}, u32[]{:S(2)}) collective-permute-start(f32[8,256,1]{1,0,2:T(8,128)} %copy.182), channel_id=1, source_target_pairs={{0,4},{4,8},{8,12},{12,16},{16,20},{20,24},{24,28},{28,0},{1,5},{5... | collective-permute-start | bytes 24584 | tf_op jit(solution)/shard_map/ppermute | solution.py:37
  168.3 3.5 copy-start.10
  168.3 18.8 %all-to-all-start.2 = ((f32[8,64,256]{2,1,0:T(8,128)}), f32[8,64,256]{2,1,0:T(8,128)S(1)}, u32[]{:S(2)}, u32[]{:S(2)}) async-start(f32[8,64,256]{2,1,0:T(8,128)} %get-tuple-element.444), calls=%async_computation.2 | async-start | bytes 1048576 | tf_op jit(solution)/shard_map/all_to_all | solution.py:167
  187.1 9.5 %copy-start.12 = (f32[8,64,256]{2,1,0:T(8,128)}, f32[8,64,256]{2,1,0:T(8,128)S(1)}, u32[]{:S(2)}) copy-start(f32[8,64,256]{2,1,0:T(8,128)S(1)} %all-to-all-done.2) | copy-start | bytes 1572868
  187.1 44.4 %all-to-all-start.3 = ((f32[8,64,256]{2,1,0:T(8,128)}), f32[8,64,256]{2,1,0:T(8,128)}, u32[]{:S(2)}, u32[]{:S(2)}) async-start(f32[8,64,256]{2,1,0:T(8,128)} %get-tuple-element.445), calls=%async_computation.3 | async-start | bytes 1048576 | tf_op jit(solution)/shard_map/all_to_all | solution.py:168
  221.1 10.2 %copy-start.17 = (pred[256,2]{0,1:T(4,128)(4,1)}, pred[256,2]{0,1:T(4,128)(4,1)S(1)}, u32[]{:S(2)}) copy-start(pred[256,2]{0,1:T(4,128)(4,1)S(1)} %reshape.394) | copy-start | bytes 1540
  231.5 20.5 %all-to-all-start.4 = ((f32[8,64,256]{2,1,0:T(8,128)}), f32[8,64,256]{2,1,0:T(8,128)S(1)}, u32[]{:S(2)}, u32[]{:S(2)}) async-start(f32[8,64,256]{2,1,0:T(8,128)} %get-tuple-element.446), calls=%async_computation.4 | async-start | bytes 1048576 | tf_op jit(solution)/shard_map/all_to_all | solution.py:169
  252.0 4.9 %copy-start.14 = (f32[8,64,256]{2,1,0:T(8,128)}, f32[8,64,256]{2,1,0:T(8,128)S(1)}, u32[]{:S(2)}) copy-start(f32[8,64,256]{2,1,0:T(8,128)S(1)} %all-to-all-done.4) | copy-start | bytes 1572868
  252.0 40.6 %all-to-all-start.5 = ((f32[8,64,256]{2,1,0:T(8,128)}), f32[8,64,256]{2,1,0:T(8,128)}, u32[]{:S(2)}, u32[]{:S(2)}) async-start(f32[8,64,256]{2,1,0:T(8,128)} %get-tuple-element.443), calls=%async_computation.5 | async-start | bytes 1048576 | tf_op jit(solution)/shard_map/all_to_all | solution.py:170
  256.9 40.2 %copy-start.16 = (s32[1024]{0:T(1024)}, s32[1024]{0:T(1024)S(1)}, u32[]{:S(2)}) copy-start(s32[1024]{0:T(1024)S(1)} %pad_clamp_fusion.3) | copy-start | bytes 12292
  256.9 5.6 %copy-start.21 = (s32[8]{0:T(128)S(1)}, s32[8]{0:T(128)}, u32[]{:S(2)}) copy-start(s32[8]{0:T(128)} %fusion.45) | copy-start | bytes 100
  256.9 3.9 copy-start.15
  260.9 27.4 %copy-start.11 = (f32[8,64,256]{2,1,0:T(8,128)S(1)}, f32[8,64,256]{2,1,0:T(8,128)}, u32[]{:S(2)}) copy-start(f32[8,64,256]{2,1,0:T(8,128)} %copy-done.10) | copy-start | bytes 1572868
  260.9 27.9 %copy-start.13 = (f32[8,64,256]{2,1,0:T(8,128)S(1)}, f32[8,64,256]{2,1,0:T(8,128)}, u32[]{:S(2)}) copy-start(f32[8,64,256]{2,1,0:T(8,128)} %copy-done.12) | copy-start | bytes 1572868
  260.9 5.1 %collective-permute-start.3 = (f32[8,1,514]{2,0,1:T(8,128)S(1)}, f32[8,1,514]{2,0,1:T(8,128)S(1)}, u32[]{:S(2)}, u32[]{:S(2)}) collective-permute-start(f32[8,1,514]{2,0,1:T(8,128)S(1)} %get-tuple-element.422), channel_id=1, source_target_pairs={{0,1},{1,2},{2,3},{3,0},{4,5},{5,6},{6,7},{7,4},{8,9},{9,10},{10,1... | collective-permute-start | bytes 49352 | tf_op jit(solution)/shard_map/ppermute | solution.py:37
  262.5 22.9 %collective-permute-start.2 = (f32[8,1,514]{2,0,1:T(8,128)}, f32[8,1,514]{2,0,1:T(8,128)}, u32[]{:S(2)}, u32[]{:S(2)}) collective-permute-start(f32[8,1,514]{2,0,1:T(8,128)} %get-tuple-element.421), channel_id=1, source_target_pairs={{1,0},{2,1},{3,2},{0,3},{5,4},{6,5},{7,6},{4,7},{9,8},{10,9},{11,1... | collective-permute-start | bytes 49352 | tf_op jit(solution)/shard_map/ppermute | solution.py:40
  292.6 66.8 %all-to-all-start.6 = ((f32[8,64,256]{2,1,0:T(8,128)}), f32[8,64,256]{2,1,0:T(8,128)}, u32[]{:S(2)}, u32[]{:S(2)}) async-start(f32[8,64,256]{2,1,0:T(8,128)} %get-tuple-element.447), calls=%async_computation.6 | async-start | bytes 1048576 | tf_op jit(solution)/shard_map/all_to_all | solution.py:171
  357.5 6.1 %copy-start.20 = (pred[8]{0:T(512)(128)(4,1)S(1)}, pred[8]{0:T(512)(128)(4,1)}, u32[]{:S(2)}) copy-start(pred[8]{0:T(512)(128)(4,1)} %compare_reduce_fusion) | copy-start | bytes 28
  365.9 20.6 %all-to-all-start.7 = ((f32[8,64,256]{2,1,0:T(8,128)}), f32[8,64,256]{2,1,0:T(8,128)}, u32[]{:S(2)}, u32[]{:S(2)}) async-start(f32[8,64,256]{2,1,0:T(8,128)} %get-tuple-element.442), calls=%async_computation.7 | async-start | bytes 1048576 | tf_op jit(solution)/shard_map/all_to_all | solution.py:198
  385.5 14.4 %copy-start.2 = (f32[1,256,512]{1,2,0:T(8,128)S(1)}, f32[1,256,512]{1,2,0:T(8,128)}, u32[]{:S(2)}) copy-start(f32[1,256,512]{1,2,0:T(8,128)} %copy.187) | copy-start | bytes 1572868
  385.5 14.4 %copy-start.3 = (f32[1,256,512]{1,2,0:T(8,128)S(1)}, f32[1,256,512]{1,2,0:T(8,128)}, u32[]{:S(2)}) copy-start(f32[1,256,512]{1,2,0:T(8,128)} %copy.188) | copy-start | bytes 1572868
  385.5 14.4 %copy-start.4 = (f32[1,256,512]{1,2,0:T(8,128)S(1)}, f32[1,256,512]{1,2,0:T(8,128)}, u32[]{:S(2)}) copy-start(f32[1,256,512]{1,2,0:T(8,128)} %copy.186) | copy-start | bytes 1572868
  385.5 14.4 %copy-start.18 = (pred[256,2]{0,1:T(4,128)(4,1)S(1)}, pred[256,2]{0,1:T(4,128)(4,1)}, u32[]{:S(2)}) copy-start(pred[256,2]{0,1:T(4,128)(4,1)} %copy-done.17) | copy-start | bytes 1540
  386.5 24.5 %all-to-all-start.9 = ((f32[8,64,256]{2,1,0:T(8,128)}), f32[8,64,256]{2,1,0:T(8,128)}, u32[]{:S(2)}, u32[]{:S(2)}) async-start(f32[8,64,256]{2,1,0:T(8,128)} %get-tuple-element.441), calls=%async_computation.9 | async-start | bytes 1048576 | tf_op jit(solution)/shard_map/all_to_all | solution.py:197
  399.9 3.1 copy-start.1
  399.9 3.2 copy-start.5
  399.9 3.4 copy-start.6
  405.3 4.4 %copy-start.7 = (f32[1,256,512]{1,2,0:T(8,128)}, f32[1,256,512]{1,2,0:T(8,128)S(1)}, u32[]{:S(2)}) copy-start(f32[1,256,512]{1,2,0:T(8,128)S(1)} %get-tuple-element.394) | copy-start | bytes 1572868
  409.7 9.1 %copy-start.19 = (pred[256,2]{0,1:T(4,128)(4,1)S(1)}, pred[256,2]{0,1:T(4,128)(4,1)}, u32[]{:S(2)}) copy-start(pred[256,2]{0,1:T(4,128)(4,1)} %reshape.391) | copy-start | bytes 1540
  411.0 20.7 %all-to-all-start.8 = ((f32[8,64,256]{2,1,0:T(8,128)}), f32[8,64,256]{2,1,0:T(8,128)}, u32[]{:S(2)}, u32[]{:S(2)}) async-start(f32[8,64,256]{2,1,0:T(8,128)} %get-tuple-element.440), calls=%async_computation.8 | async-start | bytes 1048576 | tf_op jit(solution)/shard_map/all_to_all | solution.py:196
  416.1 2.8 copy-start
  429.0 5.3 %copy-start.9 = (f32[2,256,512]{2,1,0:T(8,128)S(1)}, f32[2,256,512]{2,1,0:T(8,128)}, u32[]{:S(2)}) copy-start(f32[2,256,512]{2,1,0:T(8,128)} %param.16) | copy-start | bytes 3145732
where the time goes:
time: 439 us; the launch traced here: 436 us
  local copies, waits for them, and re-layouts  238 us (54%)
  other arithmetic  82.3 us (19%)
  starting transfers between devices  50.9 us (12%)
  waiting for transfers between devices  27.6 us (6%)
  blocking collectives  25.1 us (6%)
  loops' own time  10.2 us (2%)
    gather x144, local copies, waits for them, and re-layouts  110 us
    unnamed x72, local copies, waits for them, and re-layouts  42.9 us
    all_to_all x1, waiting for transfers between devices, shards(): lax.all_to_all(outgoing(fields[3]), 'lon', split_axis=0, concat_axis=0, t...  14.7 us
    sub x1, other arithmetic, shards(): temp + diffusion_rate * (east + west + north + south - 4.0 * temp)  14.5 us
    all_gather x1, blocking collectives, shards(): whole_row = lax.all_gather(top_row, 'lon', axis=1, tiled=True)  14.4 us
    div x32, other arithmetic, one_cycle(): (stress_two + relax_rate * viscous * shearing) / (1.0 + relax_rate)  13.6 us
    unnamed x1, blocking collectives  10.6 us
  transfers between devices with their start and end apart: 14, of which 4 were waited for; matrix products, arithmetic and copies ran while one was open for 68% of the time, Pallas kernels for 0%

commit v1 on v0

v1 whole, which is shorter than its diff:
```python
import functools

import jax
import jax.numpy as jnp
from jax import lax
from jax.experimental import pallas as pl
from jax.experimental.pallas import tpu as pltpu
from jax.sharding import PartitionSpec as P

CYCLES = 32
LANES = 128
SUBS = 8

diffusion_rate = 0.15
advect_rate = 0.5
relax_rate = 0.5
ice_step = 0.2
drag_rate = 1.0
strain_floor = 0.25
heat_rate = 0.5
freezing = -1.0

KEEP = 1.0 / (1.0 + ice_step * drag_rate)
GAIN = ice_step * KEEP
FADE = 1.0 / (1.0 + relax_rate)


def iota(dim):
    return lax.broadcasted_iota(jnp.int32, (SUBS, LANES), dim)


def ice_kernel(
    block_rows,
    block_cols,
    block_total,
    vel_hbm,
    strength_hbm,
    currents_hbm,
    temp_hbm,
    list_ref,
    vel_out,
    flux_out,
    nat,
    state,
    stress,
    fixed,
    sem_in,
    sem_out,
):
    pieces = nat.shape[1]
    group = state.shape[1]
    wide = block_cols // LANES
    per_block = block_rows // group
    cols_dev = pieces // wide
    fields = (
        vel_hbm.at[0],
        vel_hbm.at[1],
        strength_hbm,
        currents_hbm.at[0, 0],
        currents_hbm.at[1, 0],
        temp_hbm.at[0],
    )
    copies = []
    for f, field in enumerate(fields):
        for c in range(pieces):
            copy = pltpu.make_async_copy(
                field.at[:, pl.ds(c * LANES, LANES)], nat.at[f, c], sem_in.at[f, c]
            )
            copy.start()
            copies.append(copy)

    lane = iota(1)
    sub = iota(0)
    first_lane = lane == 0
    last_lane = lane == LANES - 1
    low_group = sub % per_block == 0
    high_group = sub % per_block == per_block - 1

    def strided(f, c, r):
        return nat[f, c, pl.ds(r, SUBS, stride=group), :]

    for copy in copies:
        copy.wait()

    def bring(r, carry):
        for c in range(pieces):
            state[0, r, c] = strided(0, c, r)
            state[1, r, c] = strided(1, c, r)
            fixed[0, r, c] = strided(2, c, r) * (GAIN * relax_rate * 0.5 * FADE)
            fixed[1, r, c] = strided(3, c, r) * (GAIN * drag_rate)
            fixed[2, r, c] = strided(4, c, r) * (GAIN * drag_rate)
            stress[0, r, c] = jnp.zeros((SUBS, LANES), jnp.float32)
            stress[1, r, c] = jnp.zeros((SUBS, LANES), jnp.float32)
        return carry

    lax.fori_loop(0, group, bring, 0)

    def east(row):
        result = []
        for c in range(pieces):
            if c % wide != wide - 1:
                result.append(
                    pltpu.roll(jnp.where(first_lane, row[c + 1], row[c]), LANES - 1, 1)
                )
            else:
                result.append(jnp.where(last_lane, row[c], pltpu.roll(row[c], LANES - 1, 1)))
        return result

    def west(row):
        result = []
        for c in range(pieces):
            if c % wide != 0:
                result.append(pltpu.roll(jnp.where(last_lane, row[c - 1], row[c]), 1, 1))
            else:
                result.append(jnp.where(first_lane, 0.0, pltpu.roll(row[c], 1, 1)))
        return result

    def read(ref, f, r):
        return [ref[f, r, c] for c in range(pieces)]

    def stresses(r, u, v, north_u, north_v):
        east_u = east(u)
        east_v = east(v)
        one = []
        two = []
        for c in range(pieces):
            both = u[c] + v[c]
            d = (east_u[c] + north_v[c]) - both
            h = (east_v[c] + north_u[c]) - both
            inverse = lax.rsqrt(d * d + h * h + strain_floor)
            q = fixed[0, r, c]
            w = q * inverse
            s_one = (FADE * stress[0, r, c] - q) + w * d
            s_two = FADE * stress[1, r, c] + w * h
            stress[0, r, c] = s_one
            stress[1, r, c] = s_two
            one.append(s_one)
            two.append(s_two)
        return one, two

    def moved(r, u, v, one, two, south_one, south_two):
        west_one = west(one)
        west_two = west(two)
        for c in range(pieces):
            both = one[c] + two[c]
            state[0, r, c] = (KEEP * u[c] + fixed[1, r, c]) + (
                both - (west_one[c] + south_two[c])
            )
            state[1, r, c] = (KEEP * v[c] + fixed[2, r, c]) + (
                both - (west_two[c] + south_one[c])
            )

    def one_cycle(cycle, carry):
        top = group - 1
        u = read(state, 0, 0)
        v = read(state, 1, 0)
        top_u = read(state, 0, top)
        top_v = read(state, 1, top)
        wrap_u = [
            jnp.where(high_group, t, pltpu.roll(x, SUBS - 1, 0)) for t, x in zip(top_u, u)
        ]
        wrap_v = [
            jnp.where(high_group, t, pltpu.roll(x, SUBS - 1, 0)) for t, x in zip(top_v, v)
        ]
        top_one, top_two = stresses(top, top_u, top_v, wrap_u, wrap_v)
        south_one = [jnp.where(low_group, 0.0, pltpu.roll(x, 1, 0)) for x in top_one]
        south_two = [jnp.where(low_group, 0.0, pltpu.roll(x, 1, 0)) for x in top_two]
        for r in range(top):
            if r + 1 < top:
                next_u = read(state, 0, r + 1)
                next_v = read(state, 1, r + 1)
            else:
                next_u, next_v = top_u, top_v
            one, two = stresses(r, u, v, next_u, next_v)
            moved(r, u, v, one, two, south_one, south_two)
            u, v, south_one, south_two = next_u, next_v, one, two
        moved(top, top_u, top_v, top_one, top_two, south_one, south_two)
        return carry

    lax.fori_loop(0, CYCLES, one_cycle, 0)

    entries = [list_ref[0, 0, i] for i in range(block_total)]
    masks = []
    for cb in range(cols_dev):
        mask = jnp.zeros((SUBS, LANES), jnp.int32)
        for rb in range(block_total // cols_dev):
            number = rb * cols_dev + cb
            hit = jnp.int32(0)
            for entry in entries:
                hit = jnp.where(entry == number, jnp.int32(1), hit)
            mask = jnp.where(sub // per_block == rb, hit, mask)
        masks.append(mask > 0)

    def finish(r, carry):
        for c in range(pieces):
            ice = masks[c // wide]
            u = state[0, r, c]
            v = state[1, r, c]
            rel_u = u - strided(3, c, r)
            rel_v = v - strided(4, c, r)
            speed = jnp.sqrt(rel_u * rel_u + rel_v * rel_v + 0.01)
            flux = heat_rate * speed * (freezing - strided(5, c, r))
            rows = pl.ds(r, SUBS, stride=group)
            nat[0, c, rows, :] = jnp.where(ice, u, strided(0, c, r))
            nat[1, c, rows, :] = jnp.where(ice, v, strided(1, c, r))
            nat[5, c, rows, :] = jnp.where(ice, flux, 0.0)
        return carry

    lax.fori_loop(0, group, finish, 0)
    copies = []
    for k, (f, target) in enumerate(((0, vel_out.at[0]), (1, vel_out.at[1]), (5, flux_out))):
        for c in range(pieces):
            copy = pltpu.make_async_copy(
                nat.at[f, c], target.at[:, pl.ds(c * LANES, LANES)], sem_out.at[k, c]
            )
            copy.start()
            copies.append(copy)
    for copy in copies:
        copy.wait()


def ice_step_call(ice_vel, strength, currents, temp, ice_list, block_rows, block_cols):
    rows, cols = strength.shape
    pieces = cols // LANES
    group = rows // SUBS
    block_total = ice_list.shape[-1]
    anywhere = pl.BlockSpec(memory_space=pl.ANY)
    lay = (group, pieces, SUBS, LANES)
    return pl.pallas_call(
        functools.partial(ice_kernel, block_rows, block_cols, block_total),
        out_shape=(
            jax.ShapeDtypeStruct(ice_vel.shape, jnp.float32),
            jax.ShapeDtypeStruct(strength.shape, jnp.float32),
        ),
        in_specs=[anywhere] * 4 + [pl.BlockSpec(memory_space=pltpu.SMEM)],
        out_specs=(anywhere, anywhere),
        scratch_shapes=[
            pltpu.VMEM((6, pieces, rows, LANES), jnp.float32),
            pltpu.VMEM((2,) + lay, jnp.float32),
            pltpu.VMEM((2,) + lay, jnp.float32),
            pltpu.VMEM((3,) + lay, jnp.float32),
            pltpu.SemaphoreType.DMA((6, pieces)),
            pltpu.SemaphoreType.DMA((3, pieces)),
        ],
        cost_estimate=pl.CostEstimate(
            flops=CYCLES * 40 * rows * cols,
            bytes_accessed=9 * 4 * rows * cols,
            transcendentals=CYCLES * rows * cols,
        ),
        compiler_params=pltpu.CompilerParams(vmem_limit_bytes=16 * 2**20),
        name="ice_subcycles",
    )(ice_vel, strength, currents, temp, ice_list)


STRIP = 16


def ocean_kernel(
    block_rows,
    block_cols,
    chunk,
    temp_hbm,
    currents_hbm,
    mixing_hbm,
    flux_hbm,
    west_ref,
    east_ref,
    south_ref,
    north_ref,
    mirror_ref,
    land_ref,
    out_hbm,
    temp,
    currents,
    mixing,
    flux,
    out,
    sem_in,
    sem_out,
):
    levels, held_rows, cols = temp.shape
    rows = held_rows - 2 * SUBS
    pieces = cols // LANES
    chunks = rows // chunk
    wide = block_cols // LANES
    lat_index = lax.axis_index("lat")
    lat_count = lax.axis_size("lat")

    def incoming(i):
        span = pl.ds(i * chunk, chunk)
        return (
            pltpu.make_async_copy(
                temp_hbm.at[:, span],
                temp.at[:, pl.ds(SUBS + i * chunk, chunk)],
                sem_in.at[0, i],
            ),
            pltpu.make_async_copy(
                currents_hbm.at[:, :, span], currents.at[:, :, span], sem_in.at[1, i]
            ),
            pltpu.make_async_copy(mixing_hbm.at[:, span], mixing.at[:, span], sem_in.at[2, i]),
            pltpu.make_async_copy(flux_hbm.at[span], flux.at[span], sem_in.at[3, i]),
        )

    def outgoing(i):
        span = pl.ds(i * chunk, chunk)
        return pltpu.make_async_copy(out.at[:, span], out_hbm.at[:, span], sem_out.at[i])

    for i in range(chunks):
        for copy in incoming(i):
            copy.start()

    lane = lax.broadcasted_iota(jnp.int32, (STRIP, LANES), 1)
    sub = lax.broadcasted_iota(jnp.int32, (STRIP, LANES), 0)
    first_lane = lane == 0
    last_lane = lane == LANES - 1
    low_sub = sub == 0
    high_sub = sub == STRIP - 1

    swap = (
        lax.broadcasted_iota(jnp.int32, (LANES, LANES), 0)
        + lax.broadcasted_iota(jnp.int32, (LANES, LANES), 1)
        == LANES - 1
    ).astype(jnp.float32)
    at_top = lat_index == lat_count - 1
    west_cols = jnp.transpose(west_ref[...])
    east_cols = jnp.transpose(east_ref[...])

    incoming(0)[0].wait()
    for c in range(pieces):
        span = pl.ds(c * LANES, LANES)
        across = pl.ds((pieces - 1 - c) * LANES, LANES)
        flipped = jnp.dot(
            mirror_ref[:, across],
            swap,
            precision=lax.Precision.HIGHEST,
            preferred_element_type=jnp.float32,
        )
        north = jnp.where(at_top, flipped, north_ref[:, span])
        for k in range(levels):
            temp[k, pl.ds(0, SUBS), span] = jnp.where(
                lat_index == 0,
                jnp.broadcast_to(temp[k, SUBS : SUBS + 1, span], (SUBS, LANES)),
                jnp.broadcast_to(south_ref[k : k + 1, span], (SUBS, LANES)),
            )
            temp[k, pl.ds(SUBS + rows, SUBS), span] = jnp.broadcast_to(
                north[k : k + 1], (SUBS, LANES)
            )

    for i in range(chunks):
        if i + 1 < chunks:
            incoming(i + 1)[0].wait()
        for copy in incoming(i)[1:]:
            copy.wait()
        for s in range(chunk // STRIP):
            base = i * chunk + s * STRIP
            span = pl.ds(base, STRIP)
            for c in range(pieces):
                here = pl.ds(c * LANES, LANES)
                right = []
                for k in range(levels):
                    mid = temp[k, pl.ds(SUBS + base, STRIP), here]
                    below = temp[k, pl.ds(base, SUBS), here]
                    above = temp[k, pl.ds(SUBS + base + STRIP, SUBS), here]
                    if c + 1 < pieces:
                        beyond = temp[
                            k, pl.ds(SUBS + base, STRIP), pl.ds((c + 1) * LANES, LANES)
                        ]
                    else:
                        beyond = east_cols[base : base + STRIP, k : k + 1]
                    if c > 0:
                        before = temp[
                            k, pl.ds(SUBS + base, STRIP), pl.ds((c - 1) * LANES, LANES)
                        ]
                    else:
                        before = west_cols[base : base + STRIP, k : k + 1]
                    east = pltpu.roll(jnp.where(first_lane, beyond, mid), LANES - 1, 1)
                    west = pltpu.roll(jnp.where(last_lane, before, mid), 1, 1)
                    above = jnp.concatenate([above] * (STRIP // SUBS), axis=0)
                    below = jnp.concatenate([below] * (STRIP // SUBS), axis=0)
                    north = pltpu.roll(jnp.where(low_sub, above, mid), STRIP - 1, 0)
                    south = pltpu.roll(jnp.where(high_sub, below, mid), 1, 0)
                    flow = currents[0, k, span, here] * (east - west) + currents[
                        1, k, span, here
                    ] * (north - south)
                    value = (
                        (1.0 - 4.0 * diffusion_rate) * mid
                        + diffusion_rate * ((east + west) + (north + south))
                    ) - advect_rate * flow
                    if k == 0:
                        value = value + flux[span, here]
                    right.append(value)
                ahead = jnp.ones((STRIP, LANES), jnp.float32)
                tail = None
                weights = [None] * levels
                lifts = [None] * levels
                whole = [None] * levels
                gathered = None
                for k in range(levels - 1, -1, -1):
                    if k == levels - 1:
                        tail = ahead
                        gathered = right[k]
                    else:
                        a = mixing[k, span, here]
                        tail = ahead + a * tail
                        gathered = right[k] * ahead + a * gathered
                    if k > 0:
                        lifts[k] = mixing[k - 1, span, here] * ahead
                        ahead = tail + lifts[k]
                    else:
                        ahead = tail
                    whole[k] = gathered
                    weights[k] = 1.0 / ahead
                is_land = land_ref[base // block_rows, c // wide] > 0
                x = None
                for k in range(levels):
                    x = (whole[k] if k == 0 else whole[k] + lifts[k] * x) * weights[k]
                    out[k, span, here] = jnp.where(
                        is_land, temp[k, pl.ds(SUBS + base, STRIP), here], x
                    )
        outgoing(i).start()
    for i in range(chunks):
        outgoing(i).wait()


def ocean_call(temp, currents, mixing, flux, edges, land, block_rows, block_cols):
    levels, rows, cols = temp.shape
    chunk = min(32, block_rows)
    anywhere = pl.BlockSpec(memory_space=pl.ANY)
    inside = pl.BlockSpec(memory_space=pltpu.VMEM)
    return pl.pallas_call(
        functools.partial(ocean_kernel, block_rows, block_cols, chunk),
        out_shape=jax.ShapeDtypeStruct(temp.shape, jnp.float32),
        in_specs=[anywhere] * 4 + [inside] * 5 + [pl.BlockSpec(memory_space=pltpu.SMEM)],
        out_specs=anywhere,
        scratch_shapes=[
            pltpu.VMEM((levels, rows + 2 * SUBS, cols), jnp.float32),
            pltpu.VMEM(currents.shape, jnp.float32),
            pltpu.VMEM(mixing.shape, jnp.float32),
            pltpu.VMEM(flux.shape, jnp.float32),
            pltpu.VMEM(temp.shape, jnp.float32),
            pltpu.SemaphoreType.DMA((4, rows // chunk)),
            pltpu.SemaphoreType.DMA((rows // chunk,)),
        ],
        cost_estimate=pl.CostEstimate(
            flops=45 * levels * rows * cols,
            bytes_accessed=5 * 4 * levels * rows * cols,
            transcendentals=levels * rows * cols,
        ),
        compiler_params=pltpu.CompilerParams(vmem_limit_bytes=40 * 2**20),
        name="ocean_column",
    )(temp, currents, mixing, flux, *edges, land)


def shards(temp, currents, mixing, ice_vel, strength, ice_list, land):
    levels, rows, cols = temp.shape
    lat_count = lax.axis_size("lat")
    lon_count = lax.axis_size("lon")
    block_rows = 2 * rows // lon_count
    block_cols = cols // 2
    up = [(i, (i + 1) % lon_count) for i in range(lon_count)]
    down = [(target, source) for source, target in up]
    north_up = [(i, i + 1) for i in range(lat_count - 1)]
    south_down = [(target, source) for source, target in north_up]
    across = [(i, lon_count - 1 - i) for i in range(lon_count)]
    from_west = lax.ppermute(temp[:, :, -1], "lon", up)
    from_east = lax.ppermute(temp[:, :, 0], "lon", down)
    top_row = temp[:, -1, :]
    from_south = lax.ppermute(top_row, "lat", north_up)
    from_north = lax.ppermute(temp[:, 0, :], "lat", south_down)
    mirrored = lax.ppermute(top_row, "lon", across)
    vel_out, flux = ice_step_call(
        ice_vel, strength, currents, temp, ice_list, block_rows, block_cols
    )
    temp_out = ocean_call(
        temp,
        currents,
        mixing,
        flux,
        (from_west, from_east, from_south, from_north, mirrored),
        land,
        block_rows,
        block_cols,
    )
    return (temp_out, vel_out)


def solution(mesh):
    placed = (
        P(None, "lat", "lon"),
        P(None, None, "lat", "lon"),
        P(None, "lat", "lon"),
        P(None, "lat", "lon"),
        P("lat", "lon"),
        P("lat", "lon", None),
        P("lat", "lon"),
    )
    return jax.shard_map(
        shards,
        mesh=mesh,
        in_specs=placed,
        out_specs=(P(None, "lat", "lon"), P(None, "lat", "lon")),
        check_vma=False,
    )
```

time: 439 us -> 127 us (0.29)
  local copies, waits for them, and re-layouts: 238 us -> 11.5 us
  Pallas kernels: 0 us -> 101 us
  other arithmetic: 82.3 us -> 0 us
  starting transfers between devices: 50.9 us -> 12.8 us
  waiting for transfers between devices: 27.6 us -> 0.01 us
  blocking collectives: 25.1 us -> 0 us
  loops' own time: 10.2 us -> 0 us
    gather x159 -> x0, local copies, waits for them, and re-layouts: 129 us -> none
    pallas_call x0 -> x2, Pallas kernels: none -> 101 us  [the longest x1 84.5 us: ice_step_call(): pl.pallas_call(functools.partial(ice_kernel, block_rows, block_cols, bloc...]
    all_to_all x10 -> x0, starting transfers between devices: 44.3 us -> none  [the longest x1 5.19 us: shards(): lax.all_to_all(outgoing(fields[3]), 'lon', split_axis=0, concat_axis=0, t...]
    div x129 -> x0, other arithmetic: 39.3 us -> none  [the longest x32 13.6 us: one_cycle(): (stress_two + relax_rate * viscous * shearing) / (1.0 + relax_rate)]
    unnamed x72 -> x21, local copies, waits for them, and re-layouts: 42.9 us -> 7.55 us
    slice x388 -> x2, local copies, waits for them, and re-layouts: 37.8 us -> 3.99 us  [the longest x1 2.88 us: shards(): from_east = lax.ppermute(temp[:, :, 0], 'lon', down)]
    all_to_all x10 -> x0, waiting for transfers between devices: 27.6 us -> none  [the longest x1 14.7 us: shards(): lax.all_to_all(outgoing(fields[3]), 'lon', split_axis=0, concat_axis=0, t...]
    sub x1 -> x0, other arithmetic: 14.5 us -> none  [shards(): temp + diffusion_rate * (east + west + north + south - 4.0 * temp)]
  transfers between devices with their start and end apart: 14 -> 5, of which waited for: 4 -> 0; matrix products, arithmetic and copies ran while one was open for 68% -> 4% of each run, Pallas kernels for 0% -> 67%
where the time goes in v1:
time: 127 us; the launch traced here: 126 us
  Pallas kernels  101 us (80%)
  starting transfers between devices  12.8 us (10%)
  local copies, waits for them, and re-layouts  11.5 us (9%)
    pallas_call x1, Pallas kernels, ice_step_call(): pl.pallas_call(functools.partial(ice_kernel, block_rows, block_cols, bloc...  84.5 us
    pallas_call x1, Pallas kernels, ocean_call(): pl.pallas_call(functools.partial(ocean_kernel, block_rows, block_cols, ch...  16.7 us
    unnamed x21, local copies, waits for them, and re-layouts  7.55 us
    ppermute x1, starting transfers between devices, shards(): mirrored = lax.ppermute(top_row, 'lon', across)  4.55 us
    ppermute x1, starting transfers between devices, shards(): from_south = lax.ppermute(top_row, 'lat', north_up)  3.38 us
    ppermute x1, starting transfers between devices, shards(): from_east = lax.ppermute(temp[:, :, 0], 'lon', down)  3.17 us
    slice x1, local copies, waits for them, and re-layouts, shards(): from_east = lax.ppermute(temp[:, :, 0], 'lon', down)  2.88 us
  transfers between devices with their start and end apart: 5, of which 0 were waited for; matrix products, arithmetic and copies ran while one was open for 4% of the time, Pallas kernels for 67%

profile of v1, /device:TPU:0, one launch (start us, length us, event | category | flops | bytes accessed | tf_op | source)
XLA Modules:
  0.0 126.4 jit_solution(7574311015905370955)
XLA Ops:
  0.6 0.0 copy-start.7
  0.6 0.0 copy-start.6
  0.7 0.0 copy-start.5
  0.7 0.0 copy-start.4
  0.7 1.1 fusion
  1.8 4.6 %collective-permute-start.4 = (f32[8,512]{1,0:T(8,128)S(1)}, f32[8,512]{1,0:T(8,128)S(1)}, u32[]{:S(2)}, u32[]{:S(2)}) collective-permute-start(f32[8,512]{1,0:T(8,128)S(1)} %bitcast.8), channel_id=1, source_target_pairs={{0,28},{4,24},{8,20},{12,16},{16,12},{20,8},{24,4},{28,0},{1,29},{... | collective-permute-start | bytes 49160 | tf_op jit(solution)/shard_map/ppermute | solution.py:470
  6.4 3.4 %collective-permute-start.2 = (f32[8,512]{1,0:T(8,128)S(1)}, f32[8,512]{1,0:T(8,128)S(1)}, u32[]{:S(2)}, u32[]{:S(2)}) collective-permute-start(f32[8,512]{1,0:T(8,128)S(1)} %bitcast.9), channel_id=1, source_target_pairs={{0,1},{1,2},{2,3},{4,5},{5,6},{6,7},{8,9},{9,10},{10,11},{12,13},{... | collective-permute-start | bytes 49160 | tf_op jit(solution)/shard_map/ppermute | solution.py:468
  9.8 1.3 %collective-permute-start.3 = (f32[8,512]{1,0:T(8,128)S(1)}, f32[8,512]{1,0:T(8,128)S(1)}, u32[]{:S(2)}, u32[]{:S(2)}) collective-permute-start(f32[8,512]{1,0:T(8,128)S(1)} %bitcast.10), channel_id=1, source_target_pairs={{1,0},{2,1},{3,2},{5,4},{6,5},{7,6},{9,8},{10,9},{11,10},{13,12},{... | collective-permute-start | bytes 49160 | tf_op jit(solution)/shard_map/ppermute | solution.py:469
  11.1 2.9 %fusion.1 = (f32[8,256,1]{2,1,0:T(8,128)S(1)}, f32[8,256,1]{2,1,0:T(8,128)}) fusion(f32[8,256,512]{2,1,0:T(8,128)} %temp_hbm.3), kind=kLoop, calls=%fused_computation.3 | loop fusion | bytes 32768 | tf_op jit(solution)/shard_map/slice | solution.py:466
  13.9 1.5 %copy.14 = f32[8,256,1]{1,0,2:T(8,128)S(1)} copy(f32[8,256,1]{2,1,0:T(8,128)} %get-tuple-element.9) | data formatting | bytes 16384
  15.5 0.4 collective-permute-start
  15.9 0.3 copy.15
  16.2 3.2 %collective-permute-start.1 = (f32[8,256]{1,0:T(8,128)S(1)}, f32[8,256]{1,0:T(8,128)S(1)}, u32[]{:S(2)}, u32[]{:S(2)}) collective-permute-start(f32[8,256]{1,0:T(8,128)S(1)} %bitcast.12), channel_id=1, source_target_pairs={{4,0},{8,4},{12,8},{16,12},{20,16},{24,20},{28,24},{0,28},{5,1},{9... | collective-permute-start | bytes 24584 | tf_op jit(solution)/shard_map/ppermute | solution.py:466
  19.4 0.0 copy-done.7
  19.4 0.1 copy.13.land_ref
  19.5 0.0 copy-done.6
  19.5 0.0 copy-done.5
  19.5 0.0 copy-done.4
  19.5 0.0 copy-start
  19.5 3.4 %copy-done = f32[2,8,256,512]{3,2,1,0:T(8,128)S(1)} copy-done((f32[2,8,256,512]{3,2,1,0:T(8,128)S(1)}, f32[2,8,256,512]{3,2,1,0:T(8,128)}, u32[]{:S(2)}) %copy-start) | copy-done | bytes 8388632
  22.9 0.0 copy-start.1
  22.9 2.2 %copy-done.1 = f32[8,256,512]{2,1,0:T(8,128)S(1)} copy-done((f32[8,256,512]{2,1,0:T(8,128)S(1)}, f32[8,256,512]{2,1,0:T(8,128)}, u32[]{:S(2)}) %copy-start.1) | copy-done | bytes 4194328
  25.1 0.0 copy-start.2
  25.1 0.0 copy-start.3
  25.1 84.5 %ice_subcycles.1 = (f32[2,256,512]{2,1,0:T(8,128)}, f32[256,512]{1,0:T(8,128)S(1)}) custom-call(f32[2,256,512]{2,1,0:T(8,128)S(1)} %copy-done.4, f32[256,512]{1,0:T(8,128)S(1)} %copy-done.5, f32[2,8,256,512]{3,2,1,0:T(8,128)S(1)} %copy-done, f32[8,256,512]{2,1,0:T(8,128)S(1)} %copy-done.1, s32[1,1,8]{2,1,0:T(1,128)S(1)} %copy-done.6), custom_call_target="tpu_custom_call" | custom-call | flops 167772160 | bytes 4718592 | tf_op jit(solution)/shard_map/ice_subcycles/pallas_call | solution.py:229
  109.6 0.0 collective-permute-done.west_ref
  109.6 0.0 collective-permute-done.1.east_ref
  109.6 0.0 collective-permute-done.4.mirror_ref
  109.6 0.0 collective-permute-done.2.south_ref
  109.6 0.0 collective-permute-done.3.north_ref
  109.6 0.0 copy-done.2
  109.6 0.0 copy-done.3
  109.7 16.7 %ocean_column.1 = f32[8,256,512]{2,1,0:T(8,128)} custom-call(f32[8,256,512]{2,1,0:T(8,128)S(1)} %copy-done.2, f32[2,8,256,512]{3,2,1,0:T(8,128)} %currents_hbm.3, f32[7,256,512]{2,1,0:T(8,128)S(1)} %copy-done.3, f32[256,512]{1,0:T(8,128)S(1)} %get-tuple-element.4.flux_hbm, f32[8,256]{1,0:T(8,128)S(1)} %collective-permute-done.west_ref, ...), custom_call_target="tpu_custom_call" | custom-call | flops 47185920 | bytes 20971520 | tf_op jit(solution)/shard_map/ocean_column/pallas_call | solution.py:430
  (2 shorter events, 0.0 us)
Async XLA Ops:
  0.6 18.8 %copy-start.7 = (s32[4,2]{0,1:T(2,128)S(1)}, s32[4,2]{0,1:T(2,128)}, u32[]{:S(2)}) copy-start(s32[4,2]{0,1:T(2,128)} %param.13) | copy-start | bytes 100
  0.6 18.8 %copy-start.6 = (s32[1,1,8]{2,1,0:T(1,128)S(1)}, s32[1,1,8]{2,1,0:T(1,128)}, u32[]{:S(2)}) copy-start(s32[1,1,8]{2,1,0:T(1,128)} %list_ref.1) | copy-start | bytes 100
  0.7 18.8 %copy-start.5 = (f32[256,512]{1,0:T(8,128)S(1)}, f32[256,512]{1,0:T(8,128)}, u32[]{:S(2)}) copy-start(f32[256,512]{1,0:T(8,128)} %strength_hbm.1) | copy-start | bytes 1572868
  0.7 18.8 %copy-start.4 = (f32[2,256,512]{2,1,0:T(8,128)S(1)}, f32[2,256,512]{2,1,0:T(8,128)}, u32[]{:S(2)}) copy-start(f32[2,256,512]{2,1,0:T(8,128)} %vel_hbm.1) | copy-start | bytes 3145732
  1.8 107.8 %collective-permute-start.4 = (f32[8,512]{1,0:T(8,128)S(1)}, f32[8,512]{1,0:T(8,128)S(1)}, u32[]{:S(2)}, u32[]{:S(2)}) collective-permute-start(f32[8,512]{1,0:T(8,128)S(1)} %bitcast.8), channel_id=1, source_target_pairs={{0,28},{4,24},{8,20},{12,16},{16,12},{20,8},{24,4},{28,0},{1,29},{... | collective-permute-start | bytes 49160 | tf_op jit(solution)/shard_map/ppermute | solution.py:470
  6.4 103.3 %collective-permute-start.2 = (f32[8,512]{1,0:T(8,128)S(1)}, f32[8,512]{1,0:T(8,128)S(1)}, u32[]{:S(2)}, u32[]{:S(2)}) collective-permute-start(f32[8,512]{1,0:T(8,128)S(1)} %bitcast.9), channel_id=1, source_target_pairs={{0,1},{1,2},{2,3},{4,5},{5,6},{6,7},{8,9},{9,10},{10,11},{12,13},{... | collective-permute-start | bytes 49160 | tf_op jit(solution)/shard_map/ppermute | solution.py:468
  9.8 99.9 %collective-permute-start.3 = (f32[8,512]{1,0:T(8,128)S(1)}, f32[8,512]{1,0:T(8,128)S(1)}, u32[]{:S(2)}, u32[]{:S(2)}) collective-permute-start(f32[8,512]{1,0:T(8,128)S(1)} %bitcast.10), channel_id=1, source_target_pairs={{1,0},{2,1},{3,2},{5,4},{6,5},{7,6},{9,8},{10,9},{11,10},{13,12},{... | collective-permute-start | bytes 49160 | tf_op jit(solution)/shard_map/ppermute | solution.py:469
  15.5 94.1 %collective-permute-start = (f32[8,256]{1,0:T(8,128)S(1)}, f32[8,256]{1,0:T(8,128)S(1)}, u32[]{:S(2)}, u32[]{:S(2)}) collective-permute-start(f32[8,256]{1,0:T(8,128)S(1)} %bitcast.11), channel_id=1, source_target_pairs={{0,4},{4,8},{8,12},{12,16},{16,20},{20,24},{24,28},{28,0},{1,5},{5... | collective-permute-start | bytes 24584 | tf_op jit(solution)/shard_map/ppermute | solution.py:465
  16.2 93.4 %collective-permute-start.1 = (f32[8,256]{1,0:T(8,128)S(1)}, f32[8,256]{1,0:T(8,128)S(1)}, u32[]{:S(2)}, u32[]{:S(2)}) collective-permute-start(f32[8,256]{1,0:T(8,128)S(1)} %bitcast.12), channel_id=1, source_target_pairs={{4,0},{8,4},{12,8},{16,12},{20,16},{24,20},{28,24},{0,28},{5,1},{9... | collective-permute-start | bytes 24584 | tf_op jit(solution)/shard_map/ppermute | solution.py:466
  19.5 3.4 %copy-start = (f32[2,8,256,512]{3,2,1,0:T(8,128)S(1)}, f32[2,8,256,512]{3,2,1,0:T(8,128)}, u32[]{:S(2)}) copy-start(f32[2,8,256,512]{3,2,1,0:T(8,128)} %currents_hbm.3) | copy-start | bytes 25165828
  22.9 2.2 %copy-start.1 = (f32[8,256,512]{2,1,0:T(8,128)S(1)}, f32[8,256,512]{2,1,0:T(8,128)}, u32[]{:S(2)}) copy-start(f32[8,256,512]{2,1,0:T(8,128)} %temp_hbm.3) | copy-start | bytes 12582916
  25.1 84.6 %copy-start.2 = (f32[8,256,512]{2,1,0:T(8,128)S(1)}, f32[8,256,512]{2,1,0:T(8,128)}, u32[]{:S(2)}) copy-start(f32[8,256,512]{2,1,0:T(8,128)} %temp_hbm.3) | copy-start | bytes 12582916
  25.1 84.6 %copy-start.3 = (f32[7,256,512]{2,1,0:T(8,128)S(1)}, f32[7,256,512]{2,1,0:T(8,128)}, u32[]{:S(2)}) copy-start(f32[7,256,512]{2,1,0:T(8,128)} %mixing_hbm.1) | copy-start | bytes 11010052

commit v2 on v1

--- a/solution.py
+++ b/solution.py
@@ -27,6 +27,140 @@
 
 def iota(dim):
     return lax.broadcasted_iota(jnp.int32, (SUBS, LANES), dim)
+
+
+def exact_dot(value, picks):
+    high = value.astype(jnp.bfloat16)
+    rest = value - high.astype(jnp.float32)
+    middle = rest.astype(jnp.bfloat16)
+    low = (rest - middle.astype(jnp.float32)).astype(jnp.bfloat16)
+    total = jnp.dot(low, picks, preferred_element_type=jnp.float32)
+    total = total + jnp.dot(middle, picks, preferred_element_type=jnp.float32)
+    return total + jnp.dot(high, picks, preferred_element_type=jnp.float32)
+
+
+def edge_kernel(
+    temp_hbm,
+    west_out,
+    east_out,
+    south_out,
+    north_out,
+    mirror_out,
+    columns,
+    edge_rows,
+    packed,
+    low_row,
+    high_row,
+    landed_cols,
+    landed_rows,
+    sem_in,
+    sem_send,
+    sem_recv,
+):
+    levels, rows, cols = temp_hbm.shape
+    lat = lax.axis_index("lat")
+    lon = lax.axis_index("lon")
+    lat_count = lax.axis_size("lat")
+    lon_count = lax.axis_size("lon")
+    west = {"lon": lax.rem(lon + lon_count - 1, lon_count)}
+    east = {"lon": lax.rem(lon + 1, lon_count)}
+    south = {"lat": lax.rem(lat + lat_count - 1, lat_count)}
+    north = {"lat": lax.rem(lat + 1, lat_count)}
+    mirror = {"lon": lon_count - 1 - lon}
+    barrier = pltpu.get_barrier_semaphore()
+    partners = (west, east, south, north, mirror)
+    for partner in partners:
+        pl.semaphore_signal(
+            barrier, inc=1, device_id=partner, device_id_type=pl.DeviceIdType.MESH
+        )
+    row_copies = [
+        pltpu.make_async_copy(temp_hbm.at[:, pl.ds(0, SUBS)], edge_rows.at[0], sem_in.at[0]),
+        pltpu.make_async_copy(
+            temp_hbm.at[:, pl.ds(rows - SUBS, SUBS)], edge_rows.at[1], sem_in.at[1]
+        ),
+    ]
+    col_copies = [
+        pltpu.make_async_copy(temp_hbm.at[:, :, pl.ds(0, LANES)], columns.at[0], sem_in.at[2]),
+        pltpu.make_async_copy(
+            temp_hbm.at[:, :, pl.ds(cols - LANES, LANES)], columns.at[1], sem_in.at[3]
+        ),
+    ]
+    for copy in row_copies + col_copies:
+        copy.start()
+    for copy in row_copies:
+        copy.wait()
+    for k in range(levels):
+        low_row[k : k + 1, :] = edge_rows[0, k, 0:1, :]
+        high_row[k : k + 1, :] = edge_rows[1, k, SUBS - 1 : SUBS, :]
+    pl.semaphore_wait(barrier, len(partners))
+
+    def send(slot, source, target, partner):
+        copy = pltpu.make_async_remote_copy(
+            src_ref=source,
+            dst_ref=target,
+            send_sem=sem_send.at[slot],
+            recv_sem=sem_recv.at[slot],
+            device_id=partner,
+            device_id_type=pl.DeviceIdType.MESH,
+        )
+        copy.start()
+        return copy
+
+    sent = [
+        send(0, high_row, landed_rows.at[0], north),
+        send(1, low_row, landed_rows.at[1], south),
+        send(2, high_row, landed_rows.at[2], mirror),
+    ]
+    from_lane = lax.broadcasted_iota(jnp.int32, (LANES, LANES), 0)
+    to_lane = lax.broadcasted_iota(jnp.int32, (LANES, LANES), 1)
+    for copy in col_copies:
+        copy.wait()
+    total = jnp.zeros((rows, LANES), jnp.float32)
+    for side, lane in ((0, 0), (1, LANES - 1)):
+        for k in range(levels):
+            picks = (from_lane == lane) & (to_lane == side * levels + k)
+            total = total + exact_dot(
+                columns[side, k], picks.astype(jnp.float32).astype(jnp.bfloat16)
+            )
+    packed[...] = total
+    sent.append(send(3, packed, landed_cols.at[0], east))
+    sent.append(send(4, packed, landed_cols.at[1], west))
+    for copy in sent:
+        copy.wait()
+    west_out[...] = landed_cols[0]
+    east_out[...] = landed_cols[1]
+    south_out[...] = landed_rows[0]
+    north_out[...] = landed_rows[1]
+    mirror_out[...] = landed_rows[2]
+
+
+def edges_call(temp):
+    levels, rows, cols = temp.shape
+    inside = pl.BlockSpec(memory_space=pltpu.VMEM)
+    side = jax.ShapeDtypeStruct((rows, LANES), jnp.float32)
+    line = jax.ShapeDtypeStruct((levels, cols), jnp.float32)
+    return pl.pallas_call(
+        edge_kernel,
+        out_shape=(side, side, line, line, line),
+        in_specs=[pl.BlockSpec(memory_space=pl.ANY)],
+        out_specs=(inside,) * 5,
+        scratch_shapes=[
+            pltpu.VMEM((2, levels, rows, LANES), jnp.float32),
+            pltpu.VMEM((2, levels, SUBS, cols), jnp.float32),
+            pltpu.VMEM((rows, LANES), jnp.float32),
+            pltpu.VMEM((levels, cols), jnp.float32),
+            pltpu.VMEM((levels, cols), jnp.float32),
+            pltpu.VMEM((2, rows, LANES), jnp.float32),
+            pltpu.VMEM((3, levels, cols), jnp.float32),
+            pltpu.SemaphoreType.DMA((4,)),
+            pltpu.SemaphoreType.DMA((5,)),
+            pltpu.SemaphoreType.DMA((5,)),
+        ],
+        compiler_params=pltpu.CompilerParams(
+            collective_id=0, has_side_effects=True, vmem_limit_bytes=56 * 2**20
+        ),
+        name="edge_exchange",
+    )(temp)
 
 
 def ice_kernel(
@@ -40,18 +174,21 @@
     list_ref,
     vel_out,
     flux_out,
-    nat,
-    state,
-    stress,
+    raw,
+    spread,
+    state_a,
+    state_b,
+    stress_a,
+    stress_b,
     fixed,
     sem_in,
     sem_out,
 ):
-    pieces = nat.shape[1]
-    group = state.shape[1]
-    wide = block_cols // LANES
+    rows, cols = raw.shape[1:]
+    group, pieces = state_a.shape[1:3]
     per_block = block_rows // group
-    cols_dev = pieces // wide
+    lanes_block = block_cols // pieces
+    cols_dev = cols // block_cols
     fields = (
         vel_hbm.at[0],
         vel_hbm.at[1],
@@ -60,97 +197,104 @@
         currents_hbm.at[1, 0],
         temp_hbm.at[0],
     )
-    copies = []
-    for f, field in enumerate(fields):
-        for c in range(pieces):
-            copy = pltpu.make_async_copy(
-                field.at[:, pl.ds(c * LANES, LANES)], nat.at[f, c], sem_in.at[f, c]
-            )
-            copy.start()
-            copies.append(copy)
+    copies = [
+        pltpu.make_async_copy(field, raw.at[f], sem_in.at[f]) for f, field in enumerate(fields)
+    ]
+    for copy in copies:
+        copy.start()
 
     lane = iota(1)
     sub = iota(0)
-    first_lane = lane == 0
-    last_lane = lane == LANES - 1
+    first_lane = lane % lanes_block == 0
+    last_lane = lane % lanes_block == lanes_block - 1
     low_group = sub % per_block == 0
     high_group = sub % per_block == per_block - 1
 
-    def strided(f, c, r):
-        return nat[f, c, pl.ds(r, SUBS, stride=group), :]
-
-    for copy in copies:
-        copy.wait()
+    def picks(dim):
+        near = lax.broadcasted_iota(jnp.int32, (cols, cols), dim)
+        far = lax.broadcasted_iota(jnp.int32, (cols, cols), 1 - dim)
+        return (near == pieces * (far % LANES) + far // LANES).astype(jnp.float32).astype(
+            jnp.bfloat16
+        )
+
+    to_pieces = picks(0)
+    factors = (
+        1.0,
+        1.0,
+        GAIN * relax_rate * 0.5 * FADE,
+        GAIN * drag_rate,
+        GAIN * drag_rate,
+    )
+    targets = (
+        state_a.at[0],
+        state_a.at[1],
+        fixed.at[0],
+        fixed.at[1],
+        fixed.at[2],
+    )
+    for f in range(5):
+        copies[f].wait()
+        moved_cols = exact_dot(raw[f], to_pieces)
+        for c in range(pieces):
+            spread[f, c] = moved_cols[:, c * LANES : (c + 1) * LANES]
+    copies[5].wait()
 
     def bring(r, carry):
+        for f in range(5):
+            for c in range(pieces):
+                value = spread[f, c, pl.ds(r, SUBS, stride=group), :]
+                targets[f][r, c] = value if f < 2 else value * factors[f]
         for c in range(pieces):
-            state[0, r, c] = strided(0, c, r)
-            state[1, r, c] = strided(1, c, r)
-            fixed[0, r, c] = strided(2, c, r) * (GAIN * relax_rate * 0.5 * FADE)
-            fixed[1, r, c] = strided(3, c, r) * (GAIN * drag_rate)
-            fixed[2, r, c] = strided(4, c, r) * (GAIN * drag_rate)
-            stress[0, r, c] = jnp.zeros((SUBS, LANES), jnp.float32)
-            stress[1, r, c] = jnp.zeros((SUBS, LANES), jnp.float32)
+            stress_a[0, r, c] = jnp.zeros((SUBS, LANES), jnp.float32)
+            stress_a[1, r, c] = jnp.zeros((SUBS, LANES), jnp.float32)
         return carry
 
     lax.fori_loop(0, group, bring, 0)
 
     def east(row):
-        result = []
-        for c in range(pieces):
-            if c % wide != wide - 1:
-                result.append(
-                    pltpu.roll(jnp.where(first_lane, row[c + 1], row[c]), LANES - 1, 1)
-                )
-            else:
-                result.append(jnp.where(last_lane, row[c], pltpu.roll(row[c], LANES - 1, 1)))
-        return result
+        around = jnp.where(last_lane, row[-1], pltpu.roll(row[0], LANES - 1, 1))
+        return row[1:] + [around]
 
     def west(row):
-        result = []
-        for c in range(pieces):
-            if c % wide != 0:
-                result.append(pltpu.roll(jnp.where(last_lane, row[c - 1], row[c]), 1, 1))
-            else:
-                result.append(jnp.where(first_lane, 0.0, pltpu.roll(row[c], 1, 1)))
-        return result
+        around = jnp.where(first_lane, 0.0, pltpu.roll(row[-1], 1, 1))
+        return [around] + row[:-1]
 
     def read(ref, f, r):
         return [ref[f, r, c] for c in range(pieces)]
 
-    def stresses(r, u, v, north_u, north_v):
-        east_u = east(u)
-        east_v = east(v)
-        one = []
-        two = []
-        for c in range(pieces):
-            both = u[c] + v[c]
-            d = (east_u[c] + north_v[c]) - both
-            h = (east_v[c] + north_u[c]) - both
-            inverse = lax.rsqrt(d * d + h * h + strain_floor)
-            q = fixed[0, r, c]
-            w = q * inverse
-            s_one = (FADE * stress[0, r, c] - q) + w * d
-            s_two = FADE * stress[1, r, c] + w * h
-            stress[0, r, c] = s_one
-            stress[1, r, c] = s_two
-            one.append(s_one)
-            two.append(s_two)
-        return one, two
-
-    def moved(r, u, v, one, two, south_one, south_two):
-        west_one = west(one)
-        west_two = west(two)
-        for c in range(pieces):
-            both = one[c] + two[c]
-            state[0, r, c] = (KEEP * u[c] + fixed[1, r, c]) + (
-                both - (west_one[c] + south_two[c])
-            )
-            state[1, r, c] = (KEEP * v[c] + fixed[2, r, c]) + (
-                both - (west_two[c] + south_one[c])
-            )
-
-    def one_cycle(cycle, carry):
+    def one_cycle(state, stress, state_to, stress_to):
+        def stresses(r, u, v, north_u, north_v):
+            east_u = east(u)
+            east_v = east(v)
+            one = []
+            two = []
+            for c in range(pieces):
+                both = u[c] + v[c]
+                d = (east_u[c] + north_v[c]) - both
+                h = (east_v[c] + north_u[c]) - both
+                inverse = lax.rsqrt(d * d + h * h + strain_floor)
+                q = fixed[0, r, c]
+                w = q * inverse
+                s_one = (FADE * stress[0, r, c] - q) + w * d
+                s_two = FADE * stress[1, r, c] + w * h
+                stress_to[0, r, c] = s_one
+                stress_to[1, r, c] = s_two
+                one.append(s_one)
+                two.append(s_two)
+            return one, two
+
+        def moved(r, u, v, one, two, south_one, south_two):
+            west_one = west(one)
+            west_two = west(two)
+            for c in range(pieces):
+                both = one[c] + two[c]
+                state_to[0, r, c] = (KEEP * u[c] + fixed[1, r, c]) + (
+                    both - (west_one[c] + south_two[c])
+                )
+                state_to[1, r, c] = (KEEP * v[c] + fixed[2, r, c]) + (
+                    both - (west_two[c] + south_one[c])
+                )
+
         top = group - 1
         u = read(state, 0, 0)
         v = read(state, 1, 0)
@@ -165,56 +309,64 @@
         top_one, top_two = stresses(top, top_u, top_v, wrap_u, wrap_v)
         south_one = [jnp.where(low_group, 0.0, pltpu.roll(x, 1, 0)) for x in top_one]
         south_two = [jnp.where(low_group, 0.0, pltpu.roll(x, 1, 0)) for x in top_two]
-        for r in range(top):
-            if r + 1 < top:
+        for r in range(group):
+            if r < top:
                 next_u = read(state, 0, r + 1)
                 next_v = read(state, 1, r + 1)
+                one, two = stresses(r, u, v, next_u, next_v)
             else:
-                next_u, next_v = top_u, top_v
-            one, two = stresses(r, u, v, next_u, next_v)
+                one = read(stress_to, 0, top)
+                two = read(stress_to, 1, top)
             moved(r, u, v, one, two, south_one, south_two)
             u, v, south_one, south_two = next_u, next_v, one, two
-        moved(top, top_u, top_v, top_one, top_two, south_one, south_two)
+
+    def two_cycles(cycle, carry):
+        one_cycle(state_a, stress_a, state_b, stress_b)
+        one_cycle(state_b, stress_b, state_a, stress_a)
         return carry
 
-    lax.fori_loop(0, CYCLES, one_cycle, 0)
+    lax.fori_loop(0, CYCLES // 2, two_cycles, 0)
+
+    def put(r, carry):
+        for f in range(2):
+            for c in range(pieces):
+                spread[f, c, pl.ds(r, SUBS, stride=group), :] = state_a[f, r, c]
+        return carry
+
+    lax.fori_loop(0, group, put, 0)
 
     entries = [list_ref[0, 0, i] for i in range(block_total)]
-    masks = []
-    for cb in range(cols_dev):
-        mask = jnp.zeros((SUBS, LANES), jnp.int32)
-        for rb in range(block_total // cols_dev):
-            number = rb * cols_dev + cb
-            hit = jnp.int32(0)
-            for entry in entries:
-                hit = jnp.where(entry == number, jnp.int32(1), hit)
-            mask = jnp.where(sub // per_block == rb, hit, mask)
-        masks.append(mask > 0)
-
-    def finish(r, carry):
-        for c in range(pieces):
-            ice = masks[c // wide]
-            u = state[0, r, c]
-            v = state[1, r, c]
-            rel_u = u - strided(3, c, r)
-            rel_v = v - strided(4, c, r)
-            speed = jnp.sqrt(rel_u * rel_u + rel_v * rel_v + 0.01)
-            flux = heat_rate * speed * (freezing - strided(5, c, r))
-            rows = pl.ds(r, SUBS, stride=group)
-            nat[0, c, rows, :] = jnp.where(ice, u, strided(0, c, r))
-            nat[1, c, rows, :] = jnp.where(ice, v, strided(1, c, r))
-            nat[5, c, rows, :] = jnp.where(ice, flux, 0.0)
-        return carry
-
-    lax.fori_loop(0, group, finish, 0)
+    from_pieces = picks(1)
+    new_u, new_v = (
+        exact_dot(
+            jnp.concatenate([spread[f, c] for c in range(pieces)], axis=1), from_pieces
+        )
+        for f in range(2)
+    )
+    spread_u = new_u
+    spread_v = new_v
+    for number in range(block_total):
+        hit = jnp.int32(0)
+        for entry in entries:
+            hit = jnp.where(entry == number, jnp.int32(1), hit)
+        ice = hit > 0
+        low = number // cols_dev * block_rows
+        left = number % cols_dev * block_cols
+        here = (slice(low, low + block_rows), slice(left, left + block_cols))
+        u = spread_u[here]
+        v = spread_v[here]
+        rel_u = u - raw[(3,) + here]
+        rel_v = v - raw[(4,) + here]
+        speed = jnp.sqrt(rel_u * rel_u + rel_v * rel_v + 0.01)
+        flux = heat_rate * speed * (freezing - raw[(5,) + here])
+        raw[(0,) + here] = jnp.where(ice, u, raw[(0,) + here])
+        raw[(1,) + here] = jnp.where(ice, v, raw[(1,) + here])
+        raw[(5,) + here] = jnp.where(ice, flux, 0.0)
     copies = []
     for k, (f, target) in enumerate(((0, vel_out.at[0]), (1, vel_out.at[1]), (5, flux_out))):
-        for c in range(pieces):
-            copy = pltpu.make_async_copy(
-                nat.at[f, c], target.at[:, pl.ds(c * LANES, LANES)], sem_out.at[k, c]
-            )
-            copy.start()
-            copies.append(copy)
+        copy = pltpu.make_async_copy(raw.at[f], target, sem_out.at[k])
+        copy.start()
+        copies.append(copy)
     for copy in copies:
         copy.wait()
 
@@ -235,19 +387,22 @@
         in_specs=[anywhere] * 4 + [pl.BlockSpec(memory_space=pltpu.SMEM)],
         out_specs=(anywhere, anywhere),
         scratch_shapes=[
-            pltpu.VMEM((6, pieces, rows, LANES), jnp.float32),
+            pltpu.VMEM((6, rows, cols), jnp.float32),
+            pltpu.VMEM((5, pieces, rows, LANES), jnp.float32),
+            pltpu.VMEM((2,) + lay, jnp.float32),
+            pltpu.VMEM((2,) + lay, jnp.float32),
             pltpu.VMEM((2,) + lay, jnp.float32),
             pltpu.VMEM((2,) + lay, jnp.float32),
             pltpu.VMEM((3,) + lay, jnp.float32),
-            pltpu.SemaphoreType.DMA((6, pieces)),
-            pltpu.SemaphoreType.DMA((3, pieces)),
+            pltpu.SemaphoreType.DMA((6,)),
+            pltpu.SemaphoreType.DMA((3,)),
         ],
         cost_estimate=pl.CostEstimate(
             flops=CYCLES * 40 * rows * cols,
             bytes_accessed=9 * 4 * rows * cols,
             transcendentals=CYCLES * rows * cols,
         ),
-        compiler_params=pltpu.CompilerParams(vmem_limit_bytes=16 * 2**20),
+        compiler_params=pltpu.CompilerParams(vmem_limit_bytes=56 * 2**20),
         name="ice_subcycles",
     )(ice_vel, strength, currents, temp, ice_list)
 
@@ -322,8 +477,6 @@
         == LANES - 1
     ).astype(jnp.float32)
     at_top = lat_index == lat_count - 1
-    west_cols = jnp.transpose(west_ref[...])
-    east_cols = jnp.transpose(east_ref[...])
 
     incoming(0)[0].wait()
     for c in range(pieces):
@@ -366,13 +519,15 @@
                             k, pl.ds(SUBS + base, STRIP), pl.ds((c + 1) * LANES, LANES)
                         ]
                     else:
-                        beyond = east_cols[base : base + STRIP, k : k + 1]
+                        beyond = east_ref[base : base + STRIP, k : k + 1]
                     if c > 0:
                         before = temp[
                             k, pl.ds(SUBS + base, STRIP), pl.ds((c - 1) * LANES, LANES)
                         ]
                     else:
-                        before = west_cols[base : base + STRIP, k : k + 1]
+                        before = west_ref[
+                            base : base + STRIP, levels + k : levels + k + 1
+                        ]
                     east = pltpu.roll(jnp.where(first_lane, beyond, mid), LANES - 1, 1)
                     west = pltpu.roll(jnp.where(last_lane, before, mid), 1, 1)
                     above = jnp.concatenate([above] * (STRIP // SUBS), axis=0)
@@ -446,28 +601,17 @@
             bytes_accessed=5 * 4 * levels * rows * cols,
             transcendentals=levels * rows * cols,
         ),
-        compiler_params=pltpu.CompilerParams(vmem_limit_bytes=40 * 2**20),
+        compiler_params=pltpu.CompilerParams(vmem_limit_bytes=56 * 2**20),
         name="ocean_column",
     )(temp, currents, mixing, flux, *edges, land)
 
 
 def shards(temp, currents, mixing, ice_vel, strength, ice_list, land):
     levels, rows, cols = temp.shape
-    lat_count = lax.axis_size("lat")
     lon_count = lax.axis_size("lon")
     block_rows = 2 * rows // lon_count
     block_cols = cols // 2
-    up = [(i, (i + 1) % lon_count) for i in range(lon_count)]
-    down = [(target, source) for source, target in up]
-    north_up = [(i, i + 1) for i in range(lat_count - 1)]
-    south_down = [(target, source) for source, target in north_up]
-    across = [(i, lon_count - 1 - i) for i in range(lon_count)]
-    from_west = lax.ppermute(temp[:, :, -1], "lon", up)
-    from_east = lax.ppermute(temp[:, :, 0], "lon", down)
-    top_row = temp[:, -1, :]
-    from_south = lax.ppermute(top_row, "lat", north_up)
-    from_north = lax.ppermute(temp[:, 0, :], "lat", south_down)
-    mirrored = lax.ppermute(top_row, "lon", across)
+    edges = edges_call(temp)
     vel_out, flux = ice_step_call(
         ice_vel, strength, currents, temp, ice_list, block_rows, block_cols
     )
@@ -476,7 +620,7 @@
         currents,
         mixing,
         flux,
-        (from_west, from_east, from_south, from_north, mirrored),
+        edges,
         land,
         block_rows,
         block_cols,

time: 127 us -> 59.8 us (0.47)
  Pallas kernels: 101 us -> 57.5 us
  starting transfers between devices: 12.8 us -> 0 us
  local copies, waits for them, and re-layouts: 11.5 us -> 1.34 us
    pallas_call x1, Pallas kernels: 84.5 us -> 28.8 us  [ice_step_call(): pl.pallas_call(functools.partial(ice_kernel, block_rows, block_cols, bloc...]
    ppermute x5 -> x0, starting transfers between devices: 12.8 us -> none  [the longest x1 4.55 us: shards(): mirrored = lax.ppermute(top_row, 'lon', across)]
    pallas_call x0 -> x1, Pallas kernels: none -> 11.7 us  [edges_call(): pl.pallas_call(edge_kernel, out_shape=(side, side, line, line, line), in_...]
    unnamed x21 -> x1, local copies, waits for them, and re-layouts: 7.55 us -> 1.34 us
    slice x2 -> x0, local copies, waits for them, and re-layouts: 3.99 us -> none  [the longest x1 2.88 us: shards(): from_east = lax.ppermute(temp[:, :, 0], 'lon', down)]
  transfers between devices with their start and end apart: 5 -> 0, of which waited for: 0 -> 0; matrix products, arithmetic and copies ran while one was open for 4% -> 0% of each run, Pallas kernels for 67% -> 0%
where the time goes in v2:
time: 59.8 us; the launch traced here: 59.7 us
  Pallas kernels  57.5 us (96%)
  local copies, waits for them, and re-layouts  1.34 us (2%)
  between operations  0.81 us (1%)
    pallas_call x1, Pallas kernels, ice_step_call(): pl.pallas_call(functools.partial(ice_kernel, block_rows, block_cols, bloc...  28.8 us
    pallas_call x1, Pallas kernels, ocean_call(): pl.pallas_call(functools.partial(ocean_kernel, block_rows, block_cols, ch...  17 us
    pallas_call x1, Pallas kernels, edges_call(): pl.pallas_call(edge_kernel, out_shape=(side, side, line, line, line), in_...  11.7 us
    unnamed x1, local copies, waits for them, and re-layouts  1.34 us

profile of v2, /device:TPU:0, one launch (start us, length us, event | category | flops | bytes accessed | tf_op | source)
XLA Modules:
  0.0 59.7 jit_solution(16029959692446106943)
XLA Ops:
  0.6 1.3 %copy.9.land_ref = s32[4,2]{1,0:T(4,128)} copy(s32[4,2]{0,1:T(2,128)} %param.13) | data formatting | bytes 64 | tf_op args[6]
  2.0 11.7 %edge_exchange.1 = (f32[256,128]{1,0:T(8,128)}, f32[256,128]{1,0:T(8,128)}, f32[8,512]{1,0:T(8,128)}, f32[8,512]{1,0:T(8,128)}, f32[8,512]{1,0:T(8,128)}) custom-call(f32[8,256,512]{2,1,0:T(8,128)} %temp_hbm.5), custom_call_target="tpu_custom_call" | custom-call | tf_op jit(solution)/shard_map/edge_exchange/pallas_call | solution.py:142
  13.7 28.8 %ice_subcycles.1 = (f32[2,256,512]{2,1,0:T(8,128)}, f32[256,512]{1,0:T(8,128)}) custom-call(f32[2,256,512]{2,1,0:T(8,128)} %vel_hbm.1, f32[256,512]{1,0:T(8,128)} %strength_hbm.1, f32[2,8,256,512]{3,2,1,0:T(8,128)} %currents_hbm.3, f32[8,256,512]{2,1,0:T(8,128)} %temp_hbm.5, s32[1,1,8]{2,1,0:T(1,128)} %list_ref.1), custom_call_target="tpu_custom_call" | custom-call | flops 167772160 | bytes 4718592 | tf_op jit(solution)/shard_map/ice_subcycles/pallas_call | solution.py:381
  42.5 17.0 %ocean_column.1 = f32[8,256,512]{2,1,0:T(8,128)} custom-call(f32[8,256,512]{2,1,0:T(8,128)} %temp_hbm.5, f32[2,8,256,512]{3,2,1,0:T(8,128)} %currents_hbm.3, f32[7,256,512]{2,1,0:T(8,128)} %mixing_hbm.1, f32[256,512]{1,0:T(8,128)} %get-tuple-element.9.flux_hbm, f32[256,128]{1,0:T(8,128)} %get-tuple-element.10.west_ref, ...), custom_call_target="tpu_custom_call" | custom-call | flops 47185920 | bytes 20971520 | tf_op jit(solution)/shard_map/ocean_column/pallas_call | solution.py:585
